TPU v7x, 512 devices: a whole 4x4x16 slice. The times are simulated.
512 devices in a mesh: ep: 64 (over y, z_lo, core), dp: 8 (over z_hi, x).
Axes of the slice: x: 4, y: 4, z: 16 (z_hi: 2, z_lo: 8; z = z_hi * 8 + z_lo), core: 2. Of those that a mesh axis runs over, the one named last changes fastest.
Arguments:
- hidden: bfloat16 [2, 16384, 2048], P(None, ('ep', 'dp')), may hold values from -6 to 6
- norm_gain: bfloat16 [2048], replicated, may hold values from 0.5 to 1.5
- gate_weights: float32 [2, 16384, 8], P(None, ('ep', 'dp')), may hold values from 0.05 to 1
- routes: int32 [2, 16384, 8], P(None, ('ep', 'dp')), may hold values from 0 to 63, as said below
- replica_pick: int32 [2, 16384, 8], P(None, ('ep', 'dp')), may hold values from 0 to 4095
- trainer_experts: int32 [64], replicated, may hold values from 0 to 63, each once
- hot_experts: int32 [3], replicated, may hold values from 0 to 63, as said below
- replica_hot: int32 [64], replicated, may hold values from 0 to 2, as said below
- w_gate: bfloat16 [64, 2048, 384], P('ep', 'dp'), may hold values from -0.125 to 0.125
- w_up: bfloat16 [64, 2048, 384], P('ep', 'dp'), may hold values from -0.125 to 0.125
- w_down: bfloat16 [64, 384, 2048], P('ep', None, 'dp'), may hold values from -0.3125 to 0.3125
- queries: bfloat16 [2, 16384, 4096], P(None, ('ep', 'dp')), may hold values from -6 to 6
- key_cache: bfloat16 [16384, 32, 512], P(('ep', 'dp')), may hold values from -6 to 6
- value_cache: bfloat16 [16384, 32, 512], P(('ep', 'dp')), may hold values from -6 to 6
- new_keys: bfloat16 [2, 16384, 512], P(None, ('ep', 'dp')), may hold values from -6 to 6
- new_values: bfloat16 [2, 16384, 512], P(None, ('ep', 'dp')), may hold values from -6 to 6
- cache_lengths: int32 [16384], P(('ep', 'dp')), may hold values from 2 to 32, as said below
Outputs:
- mixed: bfloat16 [2, 16384, 2048], P(None, ('ep', 'dp'))
- context: bfloat16 [2, 16384, 4096], P(None, ('ep', 'dp'))
Inputs may be any that keep to these rules, and one draw needn't show every extreme that they name: Trainer index p holds expert trainer_experts[p]; each expert once. `hot_experts`: 3 different experts, among them expert 0 and expert 64 - 1. `replica_hot`: every entry of hot_experts is named by some index. `cache_lengths`: the 32 sequences of each device include one with 32 live entries. `routes`: each row names 8 different experts; every expert is named by some row.
All inputs are finite; a program needn't handle non-finite values.
Results may differ from a plain program's by a relative error of at most 0.001.
The roundings to bfloat16 on the way count: a program that leaves them out, or rounds other values in their place, can miss the bound.
Values may be sent and summed in bfloat16 or wider, within the bound.
A program may use at most 64 MiB of HBM per device.

v0:
```python
import math

import jax
import jax.numpy as jnp
from jax import lax
from jax.sharding import PartitionSpec as P

HEADS = 32
KV_HEADS = 4
HEAD = 128
TOP = 8
CAP = 3
SLOTS = 2


norm_epsilon = 1e-06


def spread(shard, axis, root):
    mine = lax.axis_index(axis) == root
    return lax.psum(jnp.where(mine, shard, jnp.zeros_like(shard)), axis)


def scaled_norm(hidden_rows, norm_gain):
    values = hidden_rows.astype(jnp.float32)
    mean_square = jnp.mean(values * values, axis=-1, keepdims=True)
    return (values * lax.rsqrt(mean_square + norm_epsilon) * norm_gain.astype(jnp.float32)).astype(
        jnp.bfloat16
    )


def table_lookup(onehot_rows, table):
    return jnp.dot(onehot_rows, table, preferred_element_type=jnp.int32)


def attend(query_rows, key_cache, value_cache, new_keys, new_values, cache_lengths, step_index):
    rows_here = query_rows.shape[0]
    cache_len = key_cache.shape[1]
    steps_all = new_keys.shape[0]
    grouped = query_rows.reshape(rows_here, KV_HEADS, HEADS // KV_HEADS, HEAD)
    keys_cached = key_cache.reshape(rows_here, cache_len, KV_HEADS, HEAD)
    values_cached = value_cache.reshape(rows_here, cache_len, KV_HEADS, HEAD)
    keys_fresh = new_keys.reshape(steps_all, rows_here, KV_HEADS, HEAD)
    values_fresh = new_values.reshape(steps_all, rows_here, KV_HEADS, HEAD)
    score_scale = 1.0 / math.sqrt(HEAD)
    cache_scores = (
        jnp.einsum("rkgh,rckh->rkgc", grouped, keys_cached, preferred_element_type=jnp.float32)
        * score_scale
    )
    fresh_scores = (
        jnp.einsum("rkgh,srkh->rkgs", grouped, keys_fresh, preferred_element_type=jnp.float32)
        * score_scale
    )
    cache_mask = (jnp.arange(cache_len, dtype=jnp.int32)[None, :] < cache_lengths[:, None])[
        :, None, None, :
    ]
    fresh_mask = (jnp.arange(steps_all, dtype=jnp.int32) <= step_index)[None, None, None, :]
    row_max = jnp.maximum(
        jnp.max(jnp.where(cache_mask, cache_scores, -1e30), axis=-1),
        jnp.max(jnp.where(fresh_mask, fresh_scores, -1e30), axis=-1),
    )
    cache_exp = jnp.where(cache_mask, jnp.exp(cache_scores - row_max[..., None]), 0.0)
    fresh_exp = jnp.where(fresh_mask, jnp.exp(fresh_scores - row_max[..., None]), 0.0)
    row_total = jnp.sum(cache_exp, axis=-1) + jnp.sum(fresh_exp, axis=-1)
    cache_probs = (cache_exp / row_total[..., None]).astype(jnp.bfloat16)
    fresh_probs = (fresh_exp / row_total[..., None]).astype(jnp.bfloat16)
    summed = jnp.einsum(
        "rkgc,rckh->rkgh", cache_probs, values_cached, preferred_element_type=jnp.float32
    )
    summed = summed + jnp.einsum(
        "rkgs,srkh->rkgh", fresh_probs, values_fresh, preferred_element_type=jnp.float32
    )
    return summed.astype(jnp.bfloat16).reshape(rows_here, HEADS * HEAD)


def body(
    hidden,
    norm_gain,
    gate_weights,
    routes,
    replica_pick,
    trainer_experts,
    hot_experts,
    replica_hot,
    w_gate,
    w_up,
    w_down,
    queries,
    key_cache,
    value_cache,
    new_keys,
    new_values,
    cache_lengths,
):
    ep_count = lax.axis_size("ep")
    my_device = lax.axis_index("ep")
    device_ids = jnp.arange(ep_count, dtype=jnp.int32)
    expert_count = trainer_experts.shape[0]
    expert_ids = jnp.arange(expert_count, dtype=jnp.int32)
    hot_count = hot_experts.shape[0]
    hot_ids = jnp.arange(hot_count, dtype=jnp.int32)
    home_device = jnp.sum(
        jnp.where(trainer_experts[None, :] == expert_ids[:, None], device_ids[None, :], 0), axis=1
    )
    hosted = jnp.sum(
        jnp.where(replica_hot[:, None] == hot_ids[None, :], hot_experts[None, :], 0), axis=1
    )
    is_replica = (hosted[None, :] == expert_ids[:, None]).astype(jnp.int32)
    replica_order = jnp.cumsum(is_replica, axis=1) * is_replica
    copies = 1 + jnp.sum(is_replica, axis=1)
    my_hot = jnp.sum(jnp.where(device_ids == my_device, replica_hot, 0))
    own_pair = jnp.concatenate([w_gate, w_up], axis=0)
    replica_pair = jnp.zeros_like(own_pair)
    replica_down = jnp.zeros_like(w_down)
    for hot_index in range(hot_count):
        hot_expert = jnp.sum(jnp.where(hot_ids == hot_index, hot_experts, 0))
        root_device = jnp.sum(jnp.where(expert_ids == hot_expert, home_device, 0))
        sent_pair, sent_down = (
            spread(own_pair, "ep", root_device),
            spread(w_down, "ep", root_device),
        )
        wanted = my_hot == hot_index
        replica_pair = jnp.where(wanted, sent_pair, replica_pair)
        replica_down = jnp.where(wanted, sent_down, replica_down)
    slot_pair, slot_down = (
        lax.all_gather(jnp.stack([own_pair, replica_pair]), "dp", axis=2, tiled=True),
        lax.all_gather(jnp.concatenate([w_down, replica_down], axis=0), "dp", axis=2, tiled=True),
    )
    tokens_here = hidden.shape[1]
    width = hidden.shape[2]
    entries = tokens_here * TOP
    slot_total = ep_count * SLOTS
    buffer_rows = slot_total * CAP
    entry_ids = jnp.arange(entries, dtype=jnp.int32)
    token_map = (
        (entry_ids // TOP)[:, None] == jnp.arange(tokens_here, dtype=jnp.int32)[None, :]
    ).astype(jnp.float32)
    contract_first = (((0,), (0,)), ((), ()))
    mixed_steps = []
    context_steps = []
    for step_index in range(hidden.shape[0]):
        context_steps.append(
            attend(
                queries[step_index],
                key_cache,
                value_cache,
                new_keys,
                new_values,
                cache_lengths,
                step_index,
            )
        )
        normed = scaled_norm(hidden[step_index], norm_gain)
        weights_top = gate_weights[step_index]
        gates = (weights_top / jnp.sum(weights_top, axis=-1, keepdims=True)).astype(jnp.bfloat16)
        chosen = routes[step_index].reshape(entries)
        replica_picks = replica_pick[step_index].reshape(entries)
        expert_onehot = (chosen[:, None] == expert_ids[None, :]).astype(jnp.int32)
        replica_index = replica_picks % table_lookup(expert_onehot, copies)
        order_rows = table_lookup(expert_onehot, replica_order)
        replica_device = jnp.sum(
            jnp.where(order_rows == replica_index[:, None], device_ids[None, :], 0), axis=1
        )
        target = jnp.where(
            replica_index == 0, table_lookup(expert_onehot, home_device), replica_device
        )
        second_slot = (replica_index > 0).astype(jnp.int32)
        slot_index = target * SLOTS + second_slot
        slot_onehot = (
            slot_index[:, None] == jnp.arange(slot_total, dtype=jnp.int32)[None, :]
        ).astype(jnp.int32)
        slot_rank = jnp.sum(jnp.cumsum(slot_onehot, axis=0) * slot_onehot, axis=1) - 1
        is_kept = slot_rank < CAP
        row_index = second_slot * (ep_count * CAP) + target * CAP + slot_rank
        placed = (
            is_kept[:, None]
            & (row_index[:, None] == jnp.arange(buffer_rows, dtype=jnp.int32)[None, :])
        ).astype(jnp.float32)
        dispatch = lax.dot_general(placed, token_map, contract_first).astype(jnp.bfloat16)
        weighted = placed * gates.reshape(entries).astype(jnp.float32)[:, None]
        combine_map = lax.dot_general(token_map, weighted, contract_first).astype(jnp.bfloat16)
        outgoing = jnp.dot(dispatch, normed, preferred_element_type=jnp.float32).astype(
            jnp.bfloat16
        )
        outgoing = outgoing.reshape(SLOTS, ep_count, CAP, width)
        incoming = lax.all_to_all(outgoing, "ep", split_axis=1, concat_axis=1, tiled=True)
        slot_rows = incoming.reshape(SLOTS, ep_count * CAP, width)
        projected = jnp.einsum(
            "snd,skdf->sknf", slot_rows, slot_pair, preferred_element_type=jnp.float32
        )
        hidden_units = (jax.nn.silu(projected[:, 0]) * projected[:, 1]).astype(jnp.bfloat16)
        expert_out = jnp.einsum(
            "snf,sfd->snd", hidden_units, slot_down, preferred_element_type=jnp.float32
        ).astype(jnp.bfloat16)
        expert_out = expert_out.reshape(SLOTS, ep_count, CAP, width)
        returned = lax.all_to_all(
            expert_out, "ep", split_axis=1, concat_axis=1, tiled=True
        ).reshape(buffer_rows, width)
        mixed_rows = hidden[step_index].astype(jnp.float32) + jnp.dot(
            combine_map, returned, preferred_element_type=jnp.float32
        )
        mixed_steps.append(mixed_rows.astype(jnp.bfloat16))
    return (jnp.stack(mixed_steps), jnp.stack(context_steps))


def solution(mesh):
    return jax.shard_map(
        body,
        mesh=mesh,
        in_specs=(
            P(None, ("ep", "dp"), None),
            P(),
            P(None, ("ep", "dp"), None),
            P(None, ("ep", "dp"), None),
            P(None, ("ep", "dp"), None),
            P(),
            P(),
            P(),
            P("ep", "dp", None),
            P("ep", "dp", None),
            P("ep", None, "dp"),
            P(None, ("ep", "dp"), None),
            P(("ep", "dp"), None, None),
            P(("ep", "dp"), None, None),
            P(None, ("ep", "dp"), None),
            P(None, ("ep", "dp"), None),
            P(("ep", "dp")),
        ),
        out_specs=(P(None, ("ep", "dp"), None), P(None, ("ep", "dp"), None)),
        check_vma=False,
    )
```

profile of v0, /device:TPU:1, one launch (start us, length us, event | category | flops | bytes accessed | tf_op | source)
XLA Modules:
  0.0 1533.9 jit_solution(9489303480555903428)
XLA Ops:
  7.2 0.8 select_reduce_fusion.4
  8.1 1.4 fusion.152
  9.5 2.7 fusion.153
  14.0 0.9 constant_dynamic-update-slice_fusion.1
  15.0 1.0 constant_dynamic-update-slice_fusion
  16.0 1.8 broadcast_select_fusion.3
  17.7 1.0 broadcast_select_fusion
  18.8 0.6 fusion.147
  21.1 825.0 %all-reduce.3.cloned.1.call-done = (bf16[1,384,256]{2,1,0:T(8,128)(2,1)}, bf16[1,384,256]{2,1,0:T(8,128)(2,1)}, bf16[1,384,256]{2,1,0:T(8,128)(2,1)}, bf16[2,256...) async-done(((bf16[1,384,256]{2,1,0:T(8,128)(2,1)}, bf16[1,384,256]{2,1,0:T(8,128)(2,1)}, bf16[1,384,256]{2,1,0:T(8,128)(2,1)}, ...) | async-done | bytes 1769488 | tf_op jit(solution)/shard_map/psum | solution.py:21
  846.1 1.1 select_bitcast_fusion
  847.2 1.0 pad_maximum_fusion
  849.5 0.3 fusion.23
  850.9 2.1 convolution_convert_fusion.2
  853.0 4.0 reshape.209
  857.0 3.2 copy.100
  860.2 11.6 all-to-all-start.2
  872.5 0.3 fusion.22
  873.8 2.1 convolution_convert_fusion.3
  875.9 4.0 reshape.204
  879.9 3.2 copy.90
  883.1 93.7 %all-to-all-done.2 = bf16[2,64,3,2048]{3,0,2,1:T(2,128)(2,1)} async-done(((bf16[2,64,3,2048]{3,0,2,1:T(2,128)(2,1)}), bf16[2,64,3,2048]{3,0,2,1:T(2,128)(2,1)}, u32[]{:S(2)}, u32[]{:S(2)}) %all-to-all-start.2) | async-done | bytes 1572896 | tf_op jit(solution)/shard_map/all_to_all | solution.py:186
  976.8 6.8 all-to-all-start
  983.8 1.0 select_select_fusion
  984.8 0.8 pad_maximum_fusion.2
  985.6 128.7 %all-gather.3.cloned.1.call-done = bf16[2,2,2048,384]{3,2,1,0:T(8,128)(2,1)} async-done(((bf16[2,2,256,384]{3,2,1,0:T(8,128)(2,1)}), bf16[2,2,2048,384]{3,2,1,0:T(8,128)(2,1)}) %all-gather.3.cloned.1.call-update) | async-done | bytes 6291472 | tf_op jit(solution)/shard_map/all_gather | solution.py:126
  1114.3 6.1 fusion.13
  1120.5 224.6 %all-gather.5.cloned.1.call-done = bf16[2,384,2048]{2,1,0:T(8,128)(2,1)} async-done(((bf16[2,384,256]{2,1,0:T(8,128)(2,1)}), bf16[2,384,2048]{2,1,0:T(8,128)(2,1)}) %all-gather.5.cloned.1.call-update) | async-done | bytes 3145744 | tf_op jit(solution)/shard_map/all_gather | solution.py:127
  1345.1 3.3 convolution_convert_fusion
  1348.3 2.8 copy.103
  1351.1 1.1 copy-done.3
  1352.3 9.7 all-to-all-start.3
  1362.0 5.2 fusion.10
  1367.1 1.0 convolution_convert_fusion.1
  1368.2 2.8 copy.93
  1370.9 64.5 %all-to-all-done.3 = bf16[2,64,3,2048]{3,0,2,1:T(2,128)(2,1)S(1)} async-done(((bf16[2,64,3,2048]{3,0,2,1:T(2,128)(2,1)}), bf16[2,64,3,2048]{3,0,2,1:T(2,128)(2,1)S(1)}, u32[]{:S(2)}, u32[]{:S(2)}) %all-to-all-start.3) | async-done | bytes 1572896 | tf_op jit(solution)/shard_map/all_to_all | solution.py:196
  1435.5 1.1 copy-done.1
  1436.6 8.6 all-to-all-start.1
  1445.2 0.8 slice_reduce_fusion.1
  1446.1 0.7 squeeze.25
  1446.8 0.6 div.97
  1447.5 0.7 squeeze.22
  1448.2 0.7 div.92
  1449.1 0.6 reshape.216
  1449.7 0.7 iota_compare_fusion.23
  1450.5 0.4 select_reduce_fusion.3
  1450.9 0.8 select_reduce_fusion.1
  1451.7 0.4 select_reduce_fusion.2
  1452.1 1.1 fusion.36
  1453.2 0.5 fusion.176
  1453.7 0.4 fusion.37
  1454.2 0.4 fusion.115
  1454.7 0.5 fusion.19
  1455.5 0.4 fusion.114
  1456.0 0.3 copy-done.9
  1456.2 0.5 fusion.18
  1456.9 0.8 pad_maximum_fusion.1
  1457.8 2.5 copy.104
  1460.3 2.5 reshape.212
  1462.8 55.9 %all-to-all-done.1 = bf16[2,64,3,2048]{3,0,2,1:T(2,128)(2,1)} async-done(((bf16[2,64,3,2048]{3,0,2,1:T(2,128)(2,1)}), bf16[2,64,3,2048]{3,0,2,1:T(2,128)(2,1)}, u32[]{:S(2)}, u32[]{:S(2)}) %all-to-all-start.1) | async-done | bytes 1572896 | tf_op jit(solution)/shard_map/all_to_all | solution.py:196
  1518.6 2.5 copy.94
  1521.2 2.5 reshape.207
  1523.7 2.2 fusion.4
  1526.0 0.7 fusion.5
  1526.7 0.7 pad_maximum_fusion.3
  (132 shorter events, 5.3 us)
Async XLA Ops:
  7.2 1447.5 %copy-start = (bf16[32,32,512]{2,1,0:T(8,128)(2,1)S(1)}, bf16[32,32,512]{2,1,0:T(8,128)(2,1)}, u32[]{:S(2)}) copy-start(bf16[32,32,512]{2,1,0:T(8,128)(2,1)} %param.30) | copy-start | bytes 3145732
  7.2 838.9 %all-reduce.3.cloned.1.call-start = ((), (), s32[]{:S(2)}) async-start(), calls=%async_computation.6 | async-start | bytes 3538944 | tf_op jit(solution)/shard_map/psum | solution.py:21
  17.7 1.1 copy-start.30
  18.8 1095.6 %all-gather.3.cloned.1.call-start = ((), (), s32[]{:S(2)}) async-start(), calls=%async_computation.4 | async-start | bytes 7077888 | tf_op jit(solution)/shard_map/all_gather | solution.py:126
  847.2 1.1 copy-start.15
  847.2 1.3 copy-start.16
  847.2 1.5 copy-start.26
  847.2 3.3 copy-start.17
  847.2 3.5 copy-start.4
  850.9 6.1 copy-start.22
  860.2 116.5 %all-to-all-start.2 = ((bf16[2,64,3,2048]{3,0,2,1:T(2,128)(2,1)}), bf16[2,64,3,2048]{3,0,2,1:T(2,128)(2,1)}, u32[]{:S(2)}, u32[]{:S(2)}) async-start(bf16[2,64,3,2048]{3,0,2,1:T(2,128)(2,1)} %copy.100), calls=%async_computation.2 | async-start | bytes 3145728 | tf_op jit(solution)/shard_map/all_to_all | solution.py:186
  873.7 6.2 copy-start.24
  883.1 101.7 %copy-start.6 = (bf16[1,384,256]{2,1,0:T(8,128)(2,1)S(1)}, bf16[1,384,256]{2,1,0:T(8,128)(2,1)}, u32[]{:S(2)}) copy-start(bf16[1,384,256]{2,1,0:T(8,128)(2,1)} %param.27) | copy-start | bytes 589828
  976.8 374.4 %all-to-all-start = ((bf16[2,64,3,2048]{3,0,2,1:T(2,128)(2,1)}), bf16[2,64,3,2048]{3,0,2,1:T(2,128)(2,1)S(1)}, u32[]{:S(2)}, u32[]{:S(2)}) async-start(bf16[2,64,3,2048]{3,0,2,1:T(2,128)(2,1)} %copy.90), calls=%async_computation | async-start | bytes 3145728 | tf_op jit(solution)/shard_map/all_to_all | solution.py:186
  983.6 361.5 %all-gather.5.cloned.1.call-start = ((), (), s32[]{:S(2)}) async-start(), calls=%async_computation.5 | async-start | bytes 3538944 | tf_op jit(solution)/shard_map/all_gather | solution.py:127
  1351.1 1.1 copy-start.3
  1352.3 83.2 %all-to-all-start.3 = ((bf16[2,64,3,2048]{3,0,2,1:T(2,128)(2,1)}), bf16[2,64,3,2048]{3,0,2,1:T(2,128)(2,1)S(1)}, u32[]{:S(2)}, u32[]{:S(2)}) async-start(bf16[2,64,3,2048]{3,0,2,1:T(2,128)(2,1)} %bitcast.156), calls=%async_computation.3 | async-start | bytes 3145728 | tf_op jit(solution)/shard_map/all_to_all | solution.py:196
  1362.0 5.2 copy-start.29
  1435.5 1.1 copy-start.1
  1435.5 13.4 copy-start.7
  1436.6 82.0 %all-to-all-start.1 = ((bf16[2,64,3,2048]{3,0,2,1:T(2,128)(2,1)}), bf16[2,64,3,2048]{3,0,2,1:T(2,128)(2,1)}, u32[]{:S(2)}, u32[]{:S(2)}) async-start(bf16[2,64,3,2048]{3,0,2,1:T(2,128)(2,1)} %bitcast.155), calls=%async_computation.1 | async-start | bytes 3145728 | tf_op jit(solution)/shard_map/all_to_all | solution.py:196
  1445.2 3.8 copy-start.11
  1445.2 3.9 copy-start.12
  1448.9 2.0 copy-start.5
  1449.7 3.5 copy-start.27
  1451.6 1.5 copy-start.8
  1452.1 2.1 copy-start.13
  1454.7 0.8 copy-start.10
  1454.7 0.9 copy-start.14
  1454.7 0.9 copy-start.28
  1455.2 1.1 copy-start.9
  1456.2 0.7 copy-start.18
  1456.2 0.7 copy-start.19
  1456.2 0.7 copy-start.20
  1456.2 0.7 copy-start.21
  1521.2 2.5 copy-start.23
  1523.7 2.2 copy-start.2
  1523.7 2.2 copy-start.25
Sparse Core Ops, SparseCore 0:
  18.9 827.1 all-reduce.2
  849.7 264.5 all-gather.2
  1118.4 226.5 all-gather.4
where the time goes:
time: 1540 us; the launch traced here: 1530 us
  waiting for transfers between devices  1390 us (90%)
  local copies, waits for them, and re-layouts  39.7 us (3%)
  starting transfers between devices  37 us (2%)
  matrix products  28.6 us (2%)
  other arithmetic  18.3 us (1%)
  between operations  18 us (1%)
    psum x1, waiting for transfers between devices, spread(): return lax.psum(jnp.where(mine, shard, jnp.zeros_like(shard)), axis)  825 us
    all_gather x1, waiting for transfers between devices, body(): lax.all_gather(jnp.concatenate([w_down, replica_down], axis=0), 'dp', axi...  225 us
    all_gather x1, waiting for transfers between devices, body(): lax.all_gather(jnp.stack([own_pair, replica_pair]), 'dp', axis=2, tiled=T...  129 us
    all_to_all x2, waiting for transfers between devices, body(): lax.all_to_all(expert_out, 'ep', split_axis=1, concat_axis=1, tiled=True)  120 us
    all_to_all x2, waiting for transfers between devices, body(): lax.all_to_all(outgoing, 'ep', split_axis=1, concat_axis=1, tiled=True)  93.7 us
  transfers between devices with their start and end apart: 7, of which 6 were waited for; matrix products, arithmetic and copies ran while one was open for 4% of the time, Pallas kernels for 0%

commit v1 on v0

v1 whole, which is shorter than its diff:
```python
import math

import jax
import jax.numpy as jnp
from jax import lax
from jax.experimental import pallas as pl
from jax.experimental.pallas import tpu as pltpu
from jax.sharding import PartitionSpec as P

HEADS = 32
KV_HEADS = 4
HEAD = 128
TOP = 8
CAP = 3
EXPERTS = 64
FF = 384
WIDTH = 2048
ROWS = 64
SEQS = 32
CACHE = 32
FRESH = 16
GROUP = 16
PIECE = 256
GU = 16
CHUNKS = 24
LAG = 4
MESH = pl.DeviceIdType.MESH
BF16 = jnp.bfloat16
F32 = jnp.float32

norm_epsilon = 1e-06


def div(a, b):
    return lax.div(jnp.int32(a), jnp.int32(b))


def rem(a, b):
    return lax.rem(jnp.int32(a), jnp.int32(b))


def kernel(
    te_ref,
    len_ref,
    t_ref,
    hid_ref,
    wg_ref,
    wu_ref,
    wd_ref,
    q_ref,
    kc_ref,
    vc_ref,
    nk_ref,
    nv_ref,
    mixed_ref,
    ctx_ref,
    wgu,
    wdn,
    tok,
    inner,
    gv,
    pbuf,
    qbuf,
    rbuf,
    cr,
    s1,
    s2,
    xs_sem,
    xr_sem,
    ring_s,
    ring_r,
    ag_s,
    ag_r,
    c_s,
    c_r,
    s1_s,
    s1_r,
    s2_s,
    s2_r,
):
    ep = lax.axis_index("ep")
    dp = lax.axis_index("dp")
    y, zl, c = div(ep, 16), rem(div(ep, 2), 8), rem(ep, 2)
    zh, x = div(dp, 4), rem(dp, 4)
    z = zh * 8 + zl
    rho = rem(z + 16 - x, 4)
    back = rem(4 - rho, 4)

    def dev(px, py, pz, pc):
        return ((py * 8 + rem(pz, 8)) * 2 + pc, div(pz, 8) * 4 + px)

    up, down = dev(x, y, rem(z + 1, 16), c), dev(x, y, rem(z + 15, 16), c)
    twin = dev(x, y, z, 1 - c)
    xpeer = [None] + [dev(rem(x + d, 4), y, z, c) for d in (1, 2, 3)]
    ypeer = [None] + [dev(x, rem(y + d, 4), z, c) for d in (1, 2, 3)]

    barrier = pltpu.get_barrier_semaphore()
    for other in [up, down, twin] + xpeer[1:] + ypeer[1:]:
        pl.semaphore_signal(barrier, inc=1, device_id=other, device_id_type=MESH)
    pl.semaphore_wait(barrier, 9)

    def remote(src, dst, ssem, rsem, to):
        return pltpu.make_async_remote_copy(
            src_ref=src, dst_ref=dst, send_sem=ssem, recv_sem=rsem, device_id=to, device_id_type=MESH
        )

    def part_ref(q, part, xs):
        e, d = rem(q, 2), div(q, 2) * 4 + xs
        if part < 2:
            return wgu.at[e, pl.ds(pl.multiple_of(d * PIECE, PIECE), PIECE), pl.ds(part * FF, FF)]
        return wdn.at[e, d]

    def chunk_ref(q, j, is_down):
        e, half = rem(q, 2), div(q, 2)
        jj = j - GU if is_down else j
        i = div(jj, 2) if is_down else div(jj, 4)
        order = i + div(i, 2) * (5 - 2 * i)
        d = half * 4 + rem(x + order, 4)
        sub = rem(jj, 2)
        if is_down:
            return wdn.at[e, d, pl.ds(pl.multiple_of(sub * 192, 192), 192)]
        part = rem(div(jj, 2), 2)
        rows = pl.ds(pl.multiple_of(d * PIECE + sub * 128, 128), 128)
        return wgu.at[e, rows, pl.ds(pl.multiple_of(part * FF, FF), FF)]

    near_q = rem(div(z + 16 - rho - x, 4), 4)
    near_dq = rem(div(z + 16 + back - x, 4), 4)
    far_q = rem(div(z + 12 - rho - x, 4), 4)
    far_dq = rem(div(z + 20 + back - x, 4), 4)
    opp_q = rem(div(z + 8 - rho - x, 4), 4)
    source = rho == 0

    def ring_copy(q, j, is_down, flow):
        block = chunk_ref(q, j, is_down)
        return remote(block, block, ring_s.at[flow, j], ring_r.at[q, j], up if flow % 2 == 0 else down)

    def near(j, is_down):
        @pl.when(source & (rem(j, 2) == 0))
        def _():
            jj = j - GU if is_down else j
            i = div(jj, 2) if is_down else div(jj, 4)
            order = i + div(i, 2) * (5 - 2 * i)
            xs = rem(x + order, 4)
            if is_down:
                block = part_ref(near_q, 2, xs)
                remote(block, block, xs_sem.at[2], xr_sem.at[2, xs], up).wait_recv()
            else:
                part = rem(div(jj, 2), 2)
                for p in range(2):

                    @pl.when(part == p)
                    def _():
                        block = part_ref(near_q, p, xs)
                        remote(block, block, xs_sem.at[p], xr_sem.at[p, xs], up).wait_recv()

        goes_up, goes_down = ring_copy(near_q, j, is_down, 0), ring_copy(near_dq, j, is_down, 1)

        @pl.when(jnp.logical_not(source))
        def _():
            goes_up.wait_recv()

        goes_up.start()

        @pl.when(jnp.logical_not(source))
        def _():
            goes_down.wait_recv()

        goes_down.start()

    def far(j, is_down):
        goes_up, goes_down = ring_copy(far_q, j, is_down, 2), ring_copy(far_dq, j, is_down, 3)
        goes_up.wait_recv()

        @pl.when((rho < 3) | (rem(j, 2) == 0))
        def _():
            goes_up.start()

        goes_down.wait_recv()

        @pl.when((back < 3) | (rem(j, 2) == 1))
        def _():
            goes_down.start()

    def opposite(j, is_down):
        @pl.when(source)
        def _():
            ring_copy(opp_q, j, is_down, 0).wait_recv()

    def tick(t):
        for step, first in ((near, 0), (far, LAG), (opposite, 2 * LAG)):

            @pl.when((t >= first) & (t < first + GU))
            def _():
                step(t - first, False)

            @pl.when((t >= first + GU) & (t < first + CHUNKS))
            def _():
                step(t - first, True)

    tok[c, y, x] = t_ref[...]
    token_x = [remote(t_ref, tok.at[c, y, x], ag_s.at[d - 1], ag_r.at[3 - d], xpeer[d]) for d in (1, 2, 3)]
    token_y = [
        remote(tok.at[c, y], tok.at[c, y], ag_s.at[2 + d], ag_r.at[6 - d], ypeer[d]) for d in (1, 2, 3)
    ]
    token_c = [remote(tok.at[c, r], tok.at[c, r], ag_s.at[6 + r], ag_r.at[6 + r], twin) for r in range(4)]

    column = rem(zl, 4)
    my_q = zh * 2 + div(zl, 4)
    parts = (wg_ref.at[0], wu_ref.at[0], wd_ref.at[0])

    @pl.when(x == column)
    def _():
        for p in range(3):
            pltpu.make_async_copy(parts[p], part_ref(my_q, p, x), xr_sem.at[p, x]).start()

    goes_to = dev(column, y, z, c)

    def hand(p):
        return remote(parts[p], part_ref(my_q, p, x), xs_sem.at[p], xr_sem.at[p, x], goes_to)

    def hand_start(p):
        @pl.when(x != column)
        def _():
            hand(p).start()

    hand_start(0)
    hand_start(1)
    for copy in token_x:
        copy.start()
    hand_start(2)

    score_scale = 1.0 / math.sqrt(HEAD)
    column_ids = lax.broadcasted_iota(jnp.int32, (KV_HEADS * GROUP, CACHE + FRESH), 1)
    row_step = rem(div(lax.broadcasted_iota(jnp.int32, (KV_HEADS * GROUP, CACHE + FRESH), 0), 8), 2)
    fresh_seen = (column_ids >= CACHE) & (column_ids - CACHE <= row_step)

    def attend(b):
        scores, values = [], []
        for h in range(KV_HEADS):
            lanes = slice(h * HEAD, (h + 1) * HEAD)
            keys = jnp.concatenate([kc_ref[b, :, lanes], nk_ref[b, :, lanes]], axis=0)
            values.append(jnp.concatenate([vc_ref[b, :, lanes], nv_ref[b, :, lanes]], axis=0))
            scores.append(
                lax.dot_general(
                    q_ref[b, h], keys, (((1,), (1,)), ((), ())), preferred_element_type=F32
                )
            )
        live = (column_ids < jnp.minimum(len_ref[b], CACHE)) | fresh_seen
        score = jnp.where(live, jnp.concatenate(scores, axis=0) * score_scale, -1e30)
        top = jnp.max(score, axis=1, keepdims=True)
        weight = jnp.where(live, jnp.exp(score - top), 0.0)
        probs = (weight / jnp.sum(weight, axis=1, keepdims=True)).astype(BF16)
        for h in range(KV_HEADS):
            ctx_ref[b, h] = jnp.dot(
                probs[h * GROUP : (h + 1) * GROUP], values[h], preferred_element_type=F32
            ).astype(BF16)

    def attend_tick(t, carry):
        tick(t)
        attend(2 * t)
        attend(2 * t + 1)
        return carry

    lax.fori_loop(0, 3, attend_tick, 0)
    for d in (1, 2, 3):
        token_x[d - 1].wait_recv()
    for copy in token_y:
        copy.start()
    lax.fori_loop(3, 12, attend_tick, 0)
    for copy in token_y:
        copy.wait_recv()
    for copy in token_c:
        copy.start()
    lax.fori_loop(12, 16, attend_tick, 0)

    def only_tick(t, carry):
        tick(t)
        return carry

    lax.fori_loop(16, GU + 2 * LAG, only_tick, 0)
    for copy in token_c:
        copy.wait_recv()

    lane = lax.broadcasted_iota(jnp.int32, (256, 128), 1)

    def project(e, i):
        core, row = div(i, 4), rem(i, 4)
        rows = tok[core, row, :, :, pl.ds(0, WIDTH)].reshape(256, WIDTH)
        both = jnp.dot(rows, wgu[e], preferred_element_type=F32)
        gate, upper = both[:, :FF], both[:, FF:]
        inner[e, i] = (gate / (1.0 + jnp.exp(-gate)) * upper).astype(BF16)
        table = tok[core, row, :, :, pl.ds(WIDTH, 128)].reshape(256, 128).astype(F32)
        expert = te_ref[(y * 8 + x + 4 * e) * 2 + c]
        mine = jnp.sum(jnp.where(lane == expert, table, 0.0), axis=1, keepdims=True)
        gv[e, i] = jnp.broadcast_to(mine, (256, 128))

    def project_tick(n, carry):
        tick(GU + 2 * LAG + n)
        project(0, n)
        project(1, n)
        return carry

    lax.fori_loop(0, 8, project_tick, 0)

    def core_copy(n):
        return remote(pbuf.at[n % 2, 1 - c], cr.at[n], c_s.at[n], c_r.at[n], twin)

    def expand(n):
        if n >= 2:
            core_copy(n - 2).wait_send()

        def tile(core, i, carry):
            k = core * 4 + i
            total = None
            for e in range(2):
                out = jnp.dot(inner[e, k], wdn[e, n], preferred_element_type=F32)
                share = jnp.concatenate([gv[e, k], gv[e, k]], axis=1)
                part = share * out.astype(BF16).astype(F32)
                total = part if total is None else total + part
            pbuf[n % 2, core, i] = total.reshape(4, ROWS, PIECE)
            return carry

        lax.fori_loop(0, 4, lambda i, k: tile(1 - c, i, k), 0)
        core_copy(n).start()
        lax.fori_loop(0, 4, lambda i, k: tile(c, i, k), 0)

    def first_copies(n):
        out = []
        for d in (1, 2, 3):
            if n % 2 == 0:
                src, to = qbuf.at[n % 2, :, rem(x + d, 4)], xpeer[d]
            else:
                src, to = qbuf.at[n % 2, rem(y + d, 4)], ypeer[d]
            out.append(remote(src, s1.at[n, 3 - d], s1_s.at[n, d - 1], s1_r.at[n, 3 - d], to))
        return out

    def second_copies(n):
        out = []
        for d in (1, 2, 3):
            if n % 2 == 0:
                src, to = rbuf.at[n % 2, rem(y + d, 4)], ypeer[d]
            else:
                src, to = rbuf.at[n % 2, rem(x + d, 4)], xpeer[d]
            out.append(remote(src, s2.at[n, 3 - d], s2_s.at[n, d - 1], s2_r.at[n, 3 - d], to))
        return out

    def core_add(n):
        core_copy(n).wait_recv()
        if n >= 2:
            for copy in first_copies(n - 2):
                copy.wait_send()

        def add(i, carry):
            qbuf[n % 2, i] = pbuf[n % 2, c, i] + cr[n, i]
            return carry

        lax.fori_loop(0, 4, add, 0)
        for copy in first_copies(n):
            copy.start()

    def first_add(n):
        for copy in first_copies(n):
            copy.wait_recv()
        if n >= 2:
            for copy in second_copies(n - 2):
                copy.wait_send()

        def add(i, carry):
            own = qbuf[n % 2, i, x] if n % 2 == 0 else qbuf[n % 2, y, i]
            rbuf[n % 2, i] = own + s1[n, 0, i] + s1[n, 1, i] + s1[n, 2, i]
            return carry

        lax.fori_loop(0, 4, add, 0)
        for copy in second_copies(n):
            copy.start()

    def finish(n):
        for copy in second_copies(n):
            copy.wait_recv()
        own = rbuf[n % 2, y if n % 2 == 0 else x]
        total = own + s2[n, 0] + s2[n, 1] + s2[n, 2]
        lanes = slice(n * PIECE, (n + 1) * PIECE)
        mixed_ref[:, lanes] = (hid_ref[:, lanes].astype(F32) + total).astype(BF16)

    pieces = WIDTH // PIECE
    for n in range(pieces + 3):
        if n < pieces:
            expand(n)
        if 1 <= n < pieces + 1:
            core_add(n - 1)
        if 2 <= n < pieces + 2:
            first_add(n - 2)
        if n >= 3:
            finish(n - 3)

    for n in (pieces - 2, pieces - 1):
        core_copy(n).wait_send()
        for copy in first_copies(n) + second_copies(n):
            copy.wait_send()
    for copy in token_x + token_y + token_c:
        copy.wait_send()

    @pl.when(x != column)
    def _():
        for p in range(3):
            hand(p).wait_send()

    def drain(j, is_down):
        ring_copy(near_q, j, is_down, 0).wait_send()
        ring_copy(near_dq, j, is_down, 1).wait_send()

        @pl.when((rho < 3) | (rem(j, 2) == 0))
        def _():
            ring_copy(far_q, j, is_down, 2).wait_send()

        @pl.when((back < 3) | (rem(j, 2) == 1))
        def _():
            ring_copy(far_dq, j, is_down, 3).wait_send()

    def drain_gu(j, carry):
        drain(j, False)
        return carry

    def drain_down(j, carry):
        drain(j, True)
        return carry

    lax.fori_loop(0, GU, drain_gu, 0)
    lax.fori_loop(GU, CHUNKS, drain_down, 0)


def scaled_norm(hidden_rows, norm_gain):
    values = hidden_rows.astype(F32)
    mean_square = jnp.mean(values * values, axis=-1, keepdims=True)
    return (values * lax.rsqrt(mean_square + norm_epsilon) * norm_gain.astype(F32)).astype(BF16)


def gate_table(gate_weights, routes, replica_pick, hot_experts, replica_hot):
    steps, tokens, _ = routes.shape
    lanes = jnp.arange(128, dtype=jnp.int32)
    hot_ids = jnp.arange(hot_experts.shape[0], dtype=jnp.int32)
    counts = jnp.sum((replica_hot[:, None] == hot_ids[None, :]).astype(jnp.int32), axis=0)
    copies = 1 + jnp.sum(jnp.where(hot_experts[:, None] == lanes[None, :], counts[:, None], 0), axis=0)
    gates = (gate_weights / jnp.sum(gate_weights, axis=-1, keepdims=True)).astype(BF16).astype(F32)
    here = routes[..., None] == lanes
    named = jnp.any(here, axis=2)
    pick = jnp.sum(jnp.where(here, replica_pick[..., None], 0), axis=2)
    gate = jnp.sum(jnp.where(here, gates[..., None], 0.0), axis=2)
    slot = jnp.where(named, pick % copies, -1)
    order = jnp.arange(tokens, dtype=jnp.int32)
    before = (order[None, :] < order[:, None])[None, :, :, None]
    rank = jnp.sum((before & (slot[:, None, :, :] == slot[:, :, None, :])).astype(jnp.int32), axis=2)
    return jnp.where(named & (rank < CAP), gate, 0.0).astype(BF16)


def body(
    hidden,
    norm_gain,
    gate_weights,
    routes,
    replica_pick,
    trainer_experts,
    hot_experts,
    replica_hot,
    w_gate,
    w_up,
    w_down,
    queries,
    key_cache,
    value_cache,
    new_keys,
    new_values,
    cache_lengths,
):
    steps, tokens, width = hidden.shape
    table = gate_table(gate_weights, routes, replica_pick, hot_experts, replica_hot)
    rows = jnp.concatenate([scaled_norm(hidden, norm_gain), table], axis=-1).reshape(ROWS, width + 128)
    grouped = (
        queries.reshape(steps, tokens, KV_HEADS, HEADS // KV_HEADS, HEAD)
        .transpose(1, 2, 0, 3, 4)
        .reshape(tokens, KV_HEADS, GROUP, HEAD)
    )
    pad = ((0, 0), (0, FRESH - steps), (0, 0))
    fresh_keys = jnp.pad(new_keys.transpose(1, 0, 2), pad)
    fresh_values = jnp.pad(new_values.transpose(1, 0, 2), pad)
    vmem = pl.BlockSpec(memory_space=pltpu.VMEM)
    smem = pl.BlockSpec(memory_space=pltpu.SMEM)
    hbm = pl.BlockSpec(memory_space=pl.ANY)
    dma = pltpu.SemaphoreType.DMA
    mixed, context = pl.pallas_call(
        kernel,
        out_shape=(
            jax.ShapeDtypeStruct((ROWS, width), BF16),
            jax.ShapeDtypeStruct((tokens, KV_HEADS, GROUP, HEAD), BF16),
        ),
        in_specs=[smem, smem, vmem, vmem, hbm, hbm, hbm, vmem, vmem, vmem, vmem, vmem],
        out_specs=(vmem, vmem),
        scratch_shapes=[
            pltpu.VMEM((2, WIDTH, 2 * FF), BF16),
            pltpu.VMEM((2, WIDTH // PIECE, FF, PIECE), BF16),
            pltpu.VMEM((2, 4, 4, ROWS, WIDTH + 128), BF16),
            pltpu.VMEM((2, 8, 256, FF), BF16),
            pltpu.VMEM((2, 8, 256, 128), F32),
            pltpu.VMEM((2, 2, 4, 4, ROWS, PIECE), F32),
            pltpu.VMEM((2, 4, 4, ROWS, PIECE), F32),
            pltpu.VMEM((2, 4, ROWS, PIECE), F32),
            pltpu.VMEM((8, 4, 4, ROWS, PIECE), F32),
            pltpu.VMEM((8, 3, 4, ROWS, PIECE), F32),
            pltpu.VMEM((8, 3, ROWS, PIECE), F32),
            dma((3,)),
            dma((3, 4)),
            dma((4, CHUNKS)),
            dma((4, CHUNKS)),
            dma((10,)),
            dma((10,)),
            dma((8,)),
            dma((8,)),
            dma((8, 3)),
            dma((8, 3)),
            dma((8, 3)),
            dma((8, 3)),
        ],
        compiler_params=pltpu.CompilerParams(
            collective_id=0, has_side_effects=True, vmem_limit_bytes=62 * 1024 * 1024
        ),
        cost_estimate=pl.CostEstimate(flops=20_000_000_000, bytes_accessed=8_000_000, transcendentals=3_000_000),
    )(
        trainer_experts,
        cache_lengths,
        rows,
        hidden.reshape(ROWS, width),
        w_gate,
        w_up,
        w_down,
        grouped,
        key_cache,
        value_cache,
        fresh_keys,
        fresh_values,
    )
    context = (
        context.reshape(tokens, KV_HEADS, steps, HEADS // KV_HEADS, HEAD)
        .transpose(2, 0, 1, 3, 4)
        .reshape(steps, tokens, HEADS * HEAD)
    )
    return mixed.reshape(steps, tokens, width), context


def solution(mesh):
    return jax.shard_map(
        body,
        mesh=mesh,
        in_specs=(
            P(None, ("ep", "dp"), None),
            P(),
            P(None, ("ep", "dp"), None),
            P(None, ("ep", "dp"), None),
            P(None, ("ep", "dp"), None),
            P(),
            P(),
            P(),
            P("ep", "dp", None),
            P("ep", "dp", None),
            P("ep", None, "dp"),
            P(None, ("ep", "dp"), None),
            P(("ep", "dp"), None, None),
            P(("ep", "dp"), None, None),
            P(None, ("ep", "dp"), None),
            P(None, ("ep", "dp"), None),
            P(("ep", "dp")),
        ),
        out_specs=(P(None, ("ep", "dp"), None), P(None, ("ep", "dp"), None)),
        check_vma=False,
    )
```

time: 1540 us -> 904 us (0.59)
  waiting for transfers between devices: 1390 us -> 0 us
  Pallas kernels: 0 us -> 888 us
  starting transfers between devices: 37 us -> 0 us
  local copies, waits for them, and re-layouts: 39.7 us -> 9.78 us
  matrix products: 28.6 us -> 0 us
  between operations: 18 us -> 0.8 us
    pallas_call x0 -> x1, Pallas kernels: none -> 888 us  [body(): pl.pallas_call(kernel, out_shape=(jax.ShapeDtypeStruct((ROWS, width), BF1...]
    psum x1 -> x0, waiting for transfers between devices: 825 us -> none  [spread(): return lax.psum(jnp.where(mine, shard, jnp.zeros_like(shard)), axis)]
    all_gather x2 -> x0, waiting for transfers between devices: 353 us -> none  [the longest x1 225 us: body(): lax.all_gather(jnp.concatenate([w_down, replica_down], axis=0), 'dp', axi...]
    all_to_all x4 -> x0, waiting for transfers between devices: 214 us -> none  [the longest x2 120 us: body(): lax.all_to_all(expert_out, 'ep', split_axis=1, concat_axis=1, tiled=True)]
    all_to_all x4 -> x0, starting transfers between devices: 36.7 us -> none  [the longest x2 18.4 us: body(): lax.all_to_all(outgoing, 'ep', split_axis=1, concat_axis=1, tiled=True)]
    dot_general x22 -> x0, matrix products: 28.6 us -> none  [the longest x2 11.3 us: body(): jnp.einsum('snd,skdf->sknf', slot_rows, slot_pair, preferred_element_type...]
    reshape x8 -> x2, local copies, waits for them, and re-layouts: 20.1 us -> 1.96 us  [the longest x1 1.02 us: body(): context = context.reshape(tokens, KV_HEADS, steps, HEADS // KV_HEADS, HEA...]
  transfers between devices with their start and end apart: 7 -> 0, of which waited for: 6 -> 0; matrix products, arithmetic and copies ran while one was open for 4% -> 0% of each run, Pallas kernels for 0% -> 0%
where the time goes in v1:
time: 904 us; the launch traced here: 903 us
  Pallas kernels  888 us (98%)
  local copies, waits for them, and re-layouts  9.78 us (1%)
    pallas_call x1, Pallas kernels, body(): pl.pallas_call(kernel, out_shape=(jax.ShapeDtypeStruct((ROWS, width), BF1...  888 us

profile of v1, /device:TPU:1, one launch (start us, length us, event | category | flops | bytes accessed | tf_op | source)
XLA Modules:
  0.0 902.6 jit_solution(8969227880977785427)
XLA Ops:
  0.6 0.0 copy-start.9
  0.6 0.6 copy-done.9
  1.3 0.0 copy-start.10
  1.3 0.1 convert_reduce_fusion.1
  1.4 0.5 copy-done.10
  1.9 0.1 select_reduce_fusion.2
  2.0 1.1 fusion.4
  3.1 0.0 copy-start.7
  3.1 0.0 copy-start.8
  3.2 0.7 copy-done.7
  3.8 0.0 copy-done.8
  3.9 0.0 copy-start.5
  3.9 0.1 copy.28
  4.0 0.6 copy-done.5
  4.6 0.1 copy.26
  4.7 0.2 select_reduce_fusion
  4.9 0.0 copy-start.6
  4.9 0.2 fusion.7
  5.1 0.5 copy-done.6
  5.6 0.1 copy.27
  5.7 0.0 copy-start.3
  5.7 0.2 select_reduce_fusion.1
  5.9 0.0 copy-start
  5.9 0.4 fusion.8
  6.3 0.4 convert_reduce_fusion
  6.7 0.0 copy-done.3
  6.7 0.0 copy-start.4
  6.7 0.1 copy.39
  6.8 0.8 copy-done.4
  7.5 0.1 copy.38
  7.6 0.0 copy-done
  7.6 0.1 fusion.6
  7.8 0.7 pad_maximum_fusion
  8.5 0.0 copy-start.1
  8.5 0.9 pad.8.nv_ref
  9.4 0.9 pad.7.nk_ref
  10.2 0.0 copy-done.1
  10.2 0.1 copy.33
  10.3 0.9 copy.37
  11.3 888.4 %shard_map.176 = (bf16[64,2048]{1,0:T(8,128)(2,1)}, bf16[32,4,16,128]{3,2,1,0:T(8,128)(2,1)}) custom-call(s32[64]{0:T(128)} %te_ref.1, s32[32]{0:T(128)} %len_ref.1, bf16[64,2176]{1,0:T(8,128)(2,1)} %bitcast.29, bf16[64,2048]{1,0:T(8,128)(2,1)} %bitcast.25, bf16[1,256,384]{2,1,0:T(8,128)(2,1)} %wg_ref.1, bf16[1,256,384]{2,1,0:T(8,128)(2,1)} %wu_ref.1, ...), custom_call_target="tpu_custom_call" | custom-call | flops 20000000000 | bytes 8000000 | tf_op jit(solution)/shard_map/pallas_call | solution.py:490
  899.7 1.1 copy.32
  900.9 0.0 copy-start.2
  900.9 1.0 reshape.95
  901.9 0.0 copy-done.2
  901.9 0.7 copy.41
  (7 shorter events, 0.1 us)
Async XLA Ops:
  0.6 0.7 copy-start.9
  1.3 0.7 copy-start.10
  3.1 0.7 copy-start.7
  3.1 0.7 copy-start.8
  3.9 0.7 copy-start.5
  4.9 0.7 copy-start.6
  5.7 1.0 copy-start.3
  5.9 1.7 copy-start
  6.7 0.8 copy-start.4
  8.5 1.7 copy-start.1
  900.9 1.0 copy-start.2

commit v2 on v1

--- a/solution.py
+++ b/solution.py
@@ -21,9 +21,12 @@
 FRESH = 16
 GROUP = 16
 PIECE = 256
-GU = 16
-CHUNKS = 24
-LAG = 4
+GU = 32
+CHUNKS = 48
+HOP = 2
+FULL = GU + 8 * HOP
+SPLIT = 512
+DOWN_ORDER = (0, 4, 1, 5, 2, 6, 3, 7)
 MESH = pl.DeviceIdType.MESH
 BF16 = jnp.bfloat16
 F32 = jnp.float32
@@ -57,6 +60,7 @@
     wgu,
     wdn,
     tok,
+    acc,
     inner,
     gv,
     pbuf,
@@ -110,17 +114,19 @@
             return wgu.at[e, pl.ds(pl.multiple_of(d * PIECE, PIECE), PIECE), pl.ds(part * FF, FF)]
         return wdn.at[e, d]
 
+    def place(j, is_down):
+        if is_down:
+            return div(j - GU, 4), 2, rem(j, 4)
+        i = div(j, 8)
+        return rem(x + i + div(i, 2) * (5 - 2 * i), 4), rem(div(j, 4), 2), rem(j, 4)
+
     def chunk_ref(q, j, is_down):
         e, half = rem(q, 2), div(q, 2)
-        jj = j - GU if is_down else j
-        i = div(jj, 2) if is_down else div(jj, 4)
-        order = i + div(i, 2) * (5 - 2 * i)
-        d = half * 4 + rem(x + order, 4)
-        sub = rem(jj, 2)
+        xs, part, sub = place(j, is_down)
+        d = half * 4 + xs
         if is_down:
-            return wdn.at[e, d, pl.ds(pl.multiple_of(sub * 192, 192), 192)]
-        part = rem(div(jj, 2), 2)
-        rows = pl.ds(pl.multiple_of(d * PIECE + sub * 128, 128), 128)
+            return wdn.at[e, d, pl.ds(pl.multiple_of(sub * 96, 96), 96)]
+        rows = pl.ds(pl.multiple_of(d * PIECE + sub * 64, 64), 64)
         return wgu.at[e, rows, pl.ds(pl.multiple_of(part * FF, FF), FF)]
 
     near_q = rem(div(z + 16 - rho - x, 4), 4)
@@ -132,20 +138,18 @@
 
     def ring_copy(q, j, is_down, flow):
         block = chunk_ref(q, j, is_down)
-        return remote(block, block, ring_s.at[flow, j], ring_r.at[q, j], up if flow % 2 == 0 else down)
-
-    def near(j, is_down):
-        @pl.when(source & (rem(j, 2) == 0))
+        ssem = ring_s.at[flow, int(is_down)]
+        return remote(block, block, ssem, ring_r.at[q, j], up if flow % 2 == 0 else down)
+
+    def near_up(j, is_down):
+        xs, part, sub = place(j, is_down)
+
+        @pl.when(source & (sub == 0))
         def _():
-            jj = j - GU if is_down else j
-            i = div(jj, 2) if is_down else div(jj, 4)
-            order = i + div(i, 2) * (5 - 2 * i)
-            xs = rem(x + order, 4)
             if is_down:
                 block = part_ref(near_q, 2, xs)
                 remote(block, block, xs_sem.at[2], xr_sem.at[2, xs], up).wait_recv()
             else:
-                part = rem(div(jj, 2), 2)
                 for p in range(2):
 
                     @pl.when(part == p)
@@ -153,41 +157,54 @@
                         block = part_ref(near_q, p, xs)
                         remote(block, block, xs_sem.at[p], xr_sem.at[p, xs], up).wait_recv()
 
-        goes_up, goes_down = ring_copy(near_q, j, is_down, 0), ring_copy(near_dq, j, is_down, 1)
+        copy = ring_copy(near_q, j, is_down, 0)
 
         @pl.when(jnp.logical_not(source))
         def _():
-            goes_up.wait_recv()
-
-        goes_up.start()
+            copy.wait_recv()
+
+        copy.start()
+
+    def near_down(j, is_down):
+        copy = ring_copy(near_dq, j, is_down, 1)
 
         @pl.when(jnp.logical_not(source))
         def _():
-            goes_down.wait_recv()
-
-        goes_down.start()
-
-    def far(j, is_down):
-        goes_up, goes_down = ring_copy(far_q, j, is_down, 2), ring_copy(far_dq, j, is_down, 3)
-        goes_up.wait_recv()
+            copy.wait_recv()
+
+        copy.start()
+
+    def far_up(j, is_down):
+        copy = ring_copy(far_q, j, is_down, 2)
+        copy.wait_recv()
 
         @pl.when((rho < 3) | (rem(j, 2) == 0))
         def _():
-            goes_up.start()
-
-        goes_down.wait_recv()
+            copy.start()
+
+    def far_down(j, is_down):
+        copy = ring_copy(far_dq, j, is_down, 3)
+        copy.wait_recv()
 
         @pl.when((back < 3) | (rem(j, 2) == 1))
         def _():
-            goes_down.start()
+            copy.start()
 
     def opposite(j, is_down):
         @pl.when(source)
         def _():
             ring_copy(opp_q, j, is_down, 0).wait_recv()
 
+    steps = (
+        (near_up, rho * HOP),
+        (near_down, back * HOP),
+        (far_up, (rho + 4) * HOP),
+        (far_down, (back + 4) * HOP),
+        (opposite, 8 * HOP),
+    )
+
     def tick(t):
-        for step, first in ((near, 0), (far, LAG), (opposite, 2 * LAG)):
+        for step, first in steps:
 
             @pl.when((t >= first) & (t < first + GU))
             def _():
@@ -198,11 +215,20 @@
                 step(t - first, True)
 
     tok[c, y, x] = t_ref[...]
-    token_x = [remote(t_ref, tok.at[c, y, x], ag_s.at[d - 1], ag_r.at[3 - d], xpeer[d]) for d in (1, 2, 3)]
-    token_y = [
-        remote(tok.at[c, y], tok.at[c, y], ag_s.at[2 + d], ag_r.at[6 - d], ypeer[d]) for d in (1, 2, 3)
-    ]
-    token_c = [remote(tok.at[c, r], tok.at[c, r], ag_s.at[6 + r], ag_r.at[6 + r], twin) for r in range(4)]
+    first, rest = pl.ds(0, SPLIT), pl.ds(SPLIT, WIDTH + 128 - SPLIT)
+    token_1, token_2 = [], []
+    for d in (1, 2, 3):
+        token_1.append(
+            remote(t_ref.at[:, rest], tok.at[c, y, x, :, rest], ag_s.at[d - 1], ag_r.at[3 - d], xpeer[d])
+        )
+        token_1.append(
+            remote(t_ref.at[:, first], tok.at[c, y, x, :, first], ag_s.at[2 + d], ag_r.at[6 - d], ypeer[d])
+        )
+        block = tok.at[c, y, :, :, rest]
+        token_2.append(remote(block, block, ag_s.at[5 + d], ag_r.at[9 - d], ypeer[d]))
+        block = tok.at[c, :, x, :, first]
+        token_2.append(remote(block, block, ag_s.at[8 + d], ag_r.at[12 - d], xpeer[d]))
+    token_c = [remote(tok.at[c, r], tok.at[c, r], ag_s.at[12 + r], ag_r.at[12 + r], twin) for r in range(4)]
 
     column = rem(zl, 4)
     my_q = zh * 2 + div(zl, 4)
@@ -225,9 +251,8 @@
 
     hand_start(0)
     hand_start(1)
-    for copy in token_x:
+    for copy in token_1:
         copy.start()
-    hand_start(2)
 
     score_scale = 1.0 / math.sqrt(HEAD)
     column_ids = lax.broadcasted_iota(jnp.int32, (KV_HEADS * GROUP, CACHE + FRESH), 1)
@@ -257,53 +282,76 @@
 
     def attend_tick(t, carry):
         tick(t)
-        attend(2 * t)
-        attend(2 * t + 1)
+        attend(t)
         return carry
 
-    lax.fori_loop(0, 3, attend_tick, 0)
-    for d in (1, 2, 3):
-        token_x[d - 1].wait_recv()
-    for copy in token_y:
+    lax.fori_loop(0, 5, attend_tick, 0)
+    for copy in token_1:
+        copy.wait_recv()
+    for copy in token_2:
         copy.start()
-    lax.fori_loop(3, 12, attend_tick, 0)
-    for copy in token_y:
+    lax.fori_loop(5, 10, attend_tick, 0)
+    hand_start(2)
+    lax.fori_loop(10, 26, attend_tick, 0)
+    for copy in token_2:
         copy.wait_recv()
     for copy in token_c:
         copy.start()
-    lax.fori_loop(12, 16, attend_tick, 0)
-
-    def only_tick(t, carry):
-        tick(t)
-        return carry
-
-    lax.fori_loop(16, GU + 2 * LAG, only_tick, 0)
+    lax.fori_loop(26, SEQS, attend_tick, 0)
     for copy in token_c:
         copy.wait_recv()
 
     lane = lax.broadcasted_iota(jnp.int32, (256, 128), 1)
 
-    def project(e, i):
+    def product(e, i, quarters):
         core, row = div(i, 4), rem(i, 4)
-        rows = tok[core, row, :, :, pl.ds(0, WIDTH)].reshape(256, WIDTH)
-        both = jnp.dot(rows, wgu[e], preferred_element_type=F32)
+        total = None
+        for quarter in quarters:
+            xs = rem(x + (0, 1, 3, 2)[quarter], 4)
+            for half in range(2):
+                here = pl.ds(pl.multiple_of((half * 4 + xs) * PIECE, PIECE), PIECE)
+                rows = tok[core, row, :, :, here].reshape(256, PIECE)
+                part = jnp.dot(rows, wgu[e, here, :], preferred_element_type=F32)
+                total = part if total is None else total + part
+        return total
+
+    def finish_inner(e, i, quarters):
+        both = acc[e, i] + product(e, i, quarters)
         gate, upper = both[:, :FF], both[:, FF:]
         inner[e, i] = (gate / (1.0 + jnp.exp(-gate)) * upper).astype(BF16)
+
+    def share(e, i):
+        core, row = div(i, 4), rem(i, 4)
         table = tok[core, row, :, :, pl.ds(WIDTH, 128)].reshape(256, 128).astype(F32)
         expert = te_ref[(y * 8 + x + 4 * e) * 2 + c]
         mine = jnp.sum(jnp.where(lane == expert, table, 0.0), axis=1, keepdims=True)
         gv[e, i] = jnp.broadcast_to(mine, (256, 128))
 
-    def project_tick(n, carry):
-        tick(GU + 2 * LAG + n)
-        project(0, n)
-        project(1, n)
+    def first_half(n, carry):
+        tick(SEQS + n)
+        for e in range(2):
+            share(e, n)
+            acc[e, n] = product(e, n, (0, 1))
         return carry
 
-    lax.fori_loop(0, 8, project_tick, 0)
+    def third_quarter(n, carry):
+        tick(SEQS + 8 + n)
+        for e in range(2):
+            acc[e, n] += product(e, n, (2,))
+        return carry
+
+    def last_quarter(n, carry):
+        for e in range(2):
+            finish_inner(e, n, (3,))
+        tick(FULL + n)
+        return carry
+
+    lax.fori_loop(0, 8, first_half, 0)
+    lax.fori_loop(0, 8, third_quarter, 0)
+    lax.fori_loop(0, 8, last_quarter, 0)
 
     def core_copy(n):
-        return remote(pbuf.at[n % 2, 1 - c], cr.at[n], c_s.at[n], c_r.at[n], twin)
+        return remote(pbuf.at[n % 2, 1 - c], cr.at[n % 4], c_s.at[n], c_r.at[n], twin)
 
     def expand(n):
         if n >= 2:
@@ -313,35 +361,43 @@
             k = core * 4 + i
             total = None
             for e in range(2):
-                out = jnp.dot(inner[e, k], wdn[e, n], preferred_element_type=F32)
-                share = jnp.concatenate([gv[e, k], gv[e, k]], axis=1)
-                part = share * out.astype(BF16).astype(F32)
+                out = jnp.dot(inner[e, k], wdn[e, DOWN_ORDER[n]], preferred_element_type=F32)
+                weight = jnp.concatenate([gv[e, k], gv[e, k]], axis=1)
+                part = weight * out.astype(BF16).astype(F32)
                 total = part if total is None else total + part
             pbuf[n % 2, core, i] = total.reshape(4, ROWS, PIECE)
             return carry
 
         lax.fori_loop(0, 4, lambda i, k: tile(1 - c, i, k), 0)
         core_copy(n).start()
+        if n < 4:
+            tick(FULL + 8 + 2 * n)
         lax.fori_loop(0, 4, lambda i, k: tile(c, i, k), 0)
+        if n < 4:
+            tick(FULL + 9 + 2 * n)
 
     def first_copies(n):
         out = []
         for d in (1, 2, 3):
-            if n % 2 == 0:
-                src, to = qbuf.at[n % 2, :, rem(x + d, 4)], xpeer[d]
-            else:
-                src, to = qbuf.at[n % 2, rem(y + d, 4)], ypeer[d]
-            out.append(remote(src, s1.at[n, 3 - d], s1_s.at[n, d - 1], s1_r.at[n, 3 - d], to))
+            for h in range(2):
+                if h == 0:
+                    src, to = qbuf.at[n % 2, h, :, rem(x + d, 4)], xpeer[d]
+                else:
+                    src, to = qbuf.at[n % 2, h, rem(y + d, 4)], ypeer[d]
+                dst = s1.at[n % 4, h, 3 - d]
+                out.append(remote(src, dst, s1_s.at[n, h, d - 1], s1_r.at[n, h, 3 - d], to))
         return out
 
     def second_copies(n):
         out = []
         for d in (1, 2, 3):
-            if n % 2 == 0:
-                src, to = rbuf.at[n % 2, rem(y + d, 4)], ypeer[d]
-            else:
-                src, to = rbuf.at[n % 2, rem(x + d, 4)], xpeer[d]
-            out.append(remote(src, s2.at[n, 3 - d], s2_s.at[n, d - 1], s2_r.at[n, 3 - d], to))
+            for h in range(2):
+                if h == 0:
+                    src, to = rbuf.at[n % 2, h, rem(y + d, 4)], ypeer[d]
+                else:
+                    src, to = rbuf.at[n % 2, h, rem(x + d, 4)], xpeer[d]
+                dst = s2.at[n % 4, h, 3 - d]
+                out.append(remote(src, dst, s2_s.at[n, h, d - 1], s2_r.at[n, h, 3 - d], to))
         return out
 
     def core_add(n):
@@ -351,7 +407,9 @@
                 copy.wait_send()
 
         def add(i, carry):
-            qbuf[n % 2, i] = pbuf[n % 2, c, i] + cr[n, i]
+            for h in range(2):
+                lanes = slice(h * 128, (h + 1) * 128)
+                qbuf[n % 2, h, i] = pbuf[n % 2, c, i, :, :, lanes] + cr[n % 4, i, :, :, lanes]
             return carry
 
         lax.fori_loop(0, 4, add, 0)
@@ -366,8 +424,9 @@
                 copy.wait_send()
 
         def add(i, carry):
-            own = qbuf[n % 2, i, x] if n % 2 == 0 else qbuf[n % 2, y, i]
-            rbuf[n % 2, i] = own + s1[n, 0, i] + s1[n, 1, i] + s1[n, 2, i]
+            for h in range(2):
+                own = qbuf[n % 2, h, i, x] if h == 0 else qbuf[n % 2, h, y, i]
+                rbuf[n % 2, h, i] = own + s1[n % 4, h, 0, i] + s1[n % 4, h, 1, i] + s1[n % 4, h, 2, i]
             return carry
 
         lax.fori_loop(0, 4, add, 0)
@@ -377,10 +436,12 @@
     def finish(n):
         for copy in second_copies(n):
             copy.wait_recv()
-        own = rbuf[n % 2, y if n % 2 == 0 else x]
-        total = own + s2[n, 0] + s2[n, 1] + s2[n, 2]
-        lanes = slice(n * PIECE, (n + 1) * PIECE)
-        mixed_ref[:, lanes] = (hid_ref[:, lanes].astype(F32) + total).astype(BF16)
+        for h in range(2):
+            own = rbuf[n % 2, h, y if h == 0 else x]
+            total = own + s2[n % 4, h, 0] + s2[n % 4, h, 1] + s2[n % 4, h, 2]
+            begin = DOWN_ORDER[n] * PIECE + h * 128
+            lanes = slice(begin, begin + 128)
+            mixed_ref[:, lanes] = (hid_ref[:, lanes].astype(F32) + total).astype(BF16)
 
     pieces = WIDTH // PIECE
     for n in range(pieces + 3):
@@ -397,7 +458,7 @@
         core_copy(n).wait_send()
         for copy in first_copies(n) + second_copies(n):
             copy.wait_send()
-    for copy in token_x + token_y + token_c:
+    for copy in token_1 + token_2 + token_c:
         copy.wait_send()
 
     @pl.when(x != column)
@@ -405,28 +466,25 @@
         for p in range(3):
             hand(p).wait_send()
 
-    def drain(j, is_down):
-        ring_copy(near_q, j, is_down, 0).wait_send()
-        ring_copy(near_dq, j, is_down, 1).wait_send()
-
-        @pl.when((rho < 3) | (rem(j, 2) == 0))
-        def _():
-            ring_copy(far_q, j, is_down, 2).wait_send()
-
-        @pl.when((back < 3) | (rem(j, 2) == 1))
-        def _():
-            ring_copy(far_dq, j, is_down, 3).wait_send()
-
-    def drain_gu(j, carry):
-        drain(j, False)
-        return carry
-
-    def drain_down(j, carry):
-        drain(j, True)
-        return carry
-
-    lax.fori_loop(0, GU, drain_gu, 0)
-    lax.fori_loop(GU, CHUNKS, drain_down, 0)
+    def drain(flow, is_down, halves):
+        if is_down:
+            block = wdn.at[0, pl.ds(0, 2 * halves)]
+        else:
+            block = wgu.at[0, pl.ds(0, 512 * halves)]
+        remote(block, block, ring_s.at[flow, int(is_down)], ring_r.at[0, 0], up).wait_send()
+
+    for is_down in (False, True):
+        drain(0, is_down, 2)
+        drain(1, is_down, 2)
+        for flow, last in ((2, rho), (3, back)):
+
+            @pl.when(last < 3)
+            def _():
+                drain(flow, is_down, 2)
+
+            @pl.when(last == 3)
+            def _():
+                drain(flow, is_down, 1)
 
 
 def scaled_norm(hidden_rows, norm_gain):
@@ -499,26 +557,27 @@
             pltpu.VMEM((2, WIDTH, 2 * FF), BF16),
             pltpu.VMEM((2, WIDTH // PIECE, FF, PIECE), BF16),
             pltpu.VMEM((2, 4, 4, ROWS, WIDTH + 128), BF16),
+            pltpu.VMEM((2, 8, 256, 2 * FF), F32),
             pltpu.VMEM((2, 8, 256, FF), BF16),
             pltpu.VMEM((2, 8, 256, 128), F32),
             pltpu.VMEM((2, 2, 4, 4, ROWS, PIECE), F32),
-            pltpu.VMEM((2, 4, 4, ROWS, PIECE), F32),
-            pltpu.VMEM((2, 4, ROWS, PIECE), F32),
-            pltpu.VMEM((8, 4, 4, ROWS, PIECE), F32),
-            pltpu.VMEM((8, 3, 4, ROWS, PIECE), F32),
-            pltpu.VMEM((8, 3, ROWS, PIECE), F32),
+            pltpu.VMEM((2, 2, 4, 4, ROWS, 128), F32),
+            pltpu.VMEM((2, 2, 4, ROWS, 128), F32),
+            pltpu.VMEM((4, 4, 4, ROWS, PIECE), F32),
+            pltpu.VMEM((4, 2, 3, 4, ROWS, 128), F32),
+            pltpu.VMEM((4, 2, 3, ROWS, 128), F32),
             dma((3,)),
             dma((3, 4)),
+            dma((4, 2)),
             dma((4, CHUNKS)),
-            dma((4, CHUNKS)),
-            dma((10,)),
-            dma((10,)),
+            dma((16,)),
+            dma((16,)),
             dma((8,)),
             dma((8,)),
-            dma((8, 3)),
-            dma((8, 3)),
-            dma((8, 3)),
-            dma((8, 3)),
+            dma((8, 2, 3)),
+            dma((8, 2, 3)),
+            dma((8, 2, 3)),
+            dma((8, 2, 3)),
         ],
         compiler_params=pltpu.CompilerParams(
             collective_id=0, has_side_effects=True, vmem_limit_bytes=62 * 1024 * 1024

time: 904 us -> 236 us (0.26)
  Pallas kernels: 888 us -> 219 us
    pallas_call x1, Pallas kernels: 888 us -> 219 us  [body(): pl.pallas_call(kernel, out_shape=(jax.ShapeDtypeStruct((ROWS, width), BF1...]
where the time goes in v2:
time: 236 us; the launch traced here: 234 us
  Pallas kernels  219 us (93%)
  local copies, waits for them, and re-layouts  9.78 us (4%)
  other arithmetic  3.58 us (2%)
    pallas_call x1, Pallas kernels, body(): pl.pallas_call(kernel, out_shape=(jax.ShapeDtypeStruct((ROWS, width), BF1...  219 us
    unnamed x28, local copies, waits for them, and re-layouts  4.87 us

profile of v2, /device:TPU:1, one launch (start us, length us, event | category | flops | bytes accessed | tf_op | source)
XLA Modules:
  0.0 233.6 jit_solution(6769896032667737783)
XLA Ops:
  0.6 0.0 copy-start.9
  0.6 0.6 copy-done.9
  1.3 0.0 copy-start.10
  1.3 0.1 convert_reduce_fusion.1
  1.4 0.5 copy-done.10
  1.9 0.1 select_reduce_fusion.2
  2.0 1.1 fusion.4
  3.1 0.0 copy-start.7
  3.1 0.0 copy-start.8
  3.2 0.7 copy-done.7
  3.8 0.0 copy-done.8
  3.9 0.0 copy-start.5
  3.9 0.1 copy.28
  4.0 0.6 copy-done.5
  4.6 0.1 copy.26
  4.7 0.2 select_reduce_fusion
  4.9 0.0 copy-start.6
  4.9 0.2 fusion.7
  5.1 0.5 copy-done.6
  5.6 0.1 copy.27
  5.7 0.0 copy-start.3
  5.7 0.2 select_reduce_fusion.1
  5.9 0.0 copy-start
  5.9 0.4 fusion.8
  6.3 0.4 convert_reduce_fusion
  6.7 0.0 copy-done.3
  6.7 0.0 copy-start.4
  6.7 0.1 copy.39
  6.8 0.8 copy-done.4
  7.5 0.1 copy.38
  7.6 0.0 copy-done
  7.6 0.1 fusion.6
  7.8 0.7 pad_maximum_fusion
  8.5 0.0 copy-start.1
  8.5 0.9 pad.8.nv_ref
  9.4 0.9 pad.7.nk_ref
  10.2 0.0 copy-done.1
  10.2 0.1 copy.33
  10.3 0.9 copy.37
  11.3 219.5 %shard_map.176 = (bf16[64,2048]{1,0:T(8,128)(2,1)}, bf16[32,4,16,128]{3,2,1,0:T(8,128)(2,1)}) custom-call(s32[64]{0:T(128)} %te_ref.1, s32[32]{0:T(128)} %len_ref.1, bf16[64,2176]{1,0:T(8,128)(2,1)} %bitcast.29, bf16[64,2048]{1,0:T(8,128)(2,1)} %bitcast.25, bf16[1,256,384]{2,1,0:T(8,128)(2,1)} %wg_ref.1, bf16[1,256,384]{2,1,0:T(8,128)(2,1)} %wu_ref.1, ...), custom_call_target="tpu_custom_call" | custom-call | flops 20000000000 | bytes 8000000 | tf_op jit(solution)/shard_map/pallas_call | solution.py:548
  230.8 1.1 copy.32
  231.9 0.0 copy-start.2
  231.9 1.0 reshape.95
  232.9 0.0 copy-done.2
  232.9 0.7 copy.41
  (7 shorter events, 0.1 us)
Async XLA Ops:
  0.6 0.7 copy-start.9
  1.3 0.7 copy-start.10
  3.1 0.7 copy-start.7
  3.1 0.7 copy-start.8
  3.9 0.7 copy-start.5
  4.9 0.7 copy-start.6
  5.7 1.0 copy-start.3
  5.9 1.7 copy-start
  6.7 0.8 copy-start.4
  8.5 1.7 copy-start.1
  231.9 1.0 copy-start.2

commit v3 on v2

--- a/solution.py
+++ b/solution.py
@@ -67,6 +67,7 @@
     qbuf,
     rbuf,
     cr,
+    so,
     s1,
     s2,
     xs_sem,
@@ -77,6 +78,8 @@
     ag_r,
     c_s,
     c_r,
+    so_s,
+    so_r,
     s1_s,
     s1_r,
     s2_s,
@@ -285,19 +288,23 @@
         attend(t)
         return carry
 
-    lax.fori_loop(0, 5, attend_tick, 0)
+    def only_tick(t, carry):
+        tick(t)
+        return carry
+
+    lax.fori_loop(0, 14, attend_tick, 0)
     for copy in token_1:
         copy.wait_recv()
     for copy in token_2:
         copy.start()
-    lax.fori_loop(5, 10, attend_tick, 0)
     hand_start(2)
-    lax.fori_loop(10, 26, attend_tick, 0)
+    lax.fori_loop(14, SEQS, attend_tick, 0)
+    lax.fori_loop(SEQS, FULL - 12, only_tick, 0)
     for copy in token_2:
         copy.wait_recv()
     for copy in token_c:
         copy.start()
-    lax.fori_loop(26, SEQS, attend_tick, 0)
+    lax.fori_loop(FULL - 12, FULL - 6, only_tick, 0)
     for copy in token_c:
         copy.wait_recv()
 
@@ -328,27 +335,34 @@
         gv[e, i] = jnp.broadcast_to(mine, (256, 128))
 
     def first_half(n, carry):
-        tick(SEQS + n)
-        for e in range(2):
-            share(e, n)
-            acc[e, n] = product(e, n, (0, 1))
+        tick(FULL - 6 + n)
+        for i in range(2):
+            for e in range(2):
+                share(e, 2 * n + i)
+                acc[e, 2 * n + i] = product(e, 2 * n + i, (0, 1))
         return carry
 
     def third_quarter(n, carry):
-        tick(SEQS + 8 + n)
-        for e in range(2):
-            acc[e, n] += product(e, n, (2,))
+        tick(FULL - 2 + n)
+
+        def rows(i, carry):
+            for e in range(2):
+                acc[e, i] += product(e, i, (2,))
+            return carry
+
+        lax.fori_loop(4 * n, 4 * n + 4, rows, 0)
         return carry
 
     def last_quarter(n, carry):
-        for e in range(2):
-            finish_inner(e, n, (3,))
+        for i in range(2):
+            for e in range(2):
+                finish_inner(e, 2 * n + i, (3,))
         tick(FULL + n)
         return carry
 
-    lax.fori_loop(0, 8, first_half, 0)
-    lax.fori_loop(0, 8, third_quarter, 0)
-    lax.fori_loop(0, 8, last_quarter, 0)
+    lax.fori_loop(0, 4, first_half, 0)
+    lax.fori_loop(0, 2, third_quarter, 0)
+    lax.fori_loop(0, 4, last_quarter, 0)
 
     def core_copy(n):
         return remote(pbuf.at[n % 2, 1 - c], cr.at[n % 4], c_s.at[n], c_r.at[n], twin)
@@ -370,22 +384,37 @@
 
         lax.fori_loop(0, 4, lambda i, k: tile(1 - c, i, k), 0)
         core_copy(n).start()
-        if n < 4:
-            tick(FULL + 8 + 2 * n)
+        if n < 6:
+            tick(FULL + 4 + 2 * n)
         lax.fori_loop(0, 4, lambda i, k: tile(c, i, k), 0)
-        if n < 4:
-            tick(FULL + 9 + 2 * n)
+        if n < 6:
+            tick(FULL + 5 + 2 * n)
+
+    def block(n, h, k, rows):
+        return qbuf.at[n % 3, h, rows, k] if h == 0 else qbuf.at[n % 3, h, k, rows]
+
+    def along(h, d):
+        return (rem(x + d, 4), xpeer[d]) if h == 0 else (rem(y + d, 4), ypeer[d])
+
+    def opposite_copies(n):
+        out = []
+        for h in range(2):
+            across, _ = along(h, 2)
+            for side, d in ((0, 1), (1, 3)):
+                src = block(n, h, across, pl.ds(2 * side, 2))
+                dst = so.at[n % 4, h, side]
+                out.append(remote(src, dst, so_s.at[n, h, side], so_r.at[n, h, side], along(h, d)[1]))
+        return out
 
     def first_copies(n):
         out = []
-        for d in (1, 2, 3):
-            for h in range(2):
-                if h == 0:
-                    src, to = qbuf.at[n % 2, h, :, rem(x + d, 4)], xpeer[d]
-                else:
-                    src, to = qbuf.at[n % 2, h, rem(y + d, 4)], ypeer[d]
-                dst = s1.at[n % 4, h, 3 - d]
-                out.append(remote(src, dst, s1_s.at[n, h, d - 1], s1_r.at[n, h, 3 - d], to))
+        for h in range(2):
+            for side, d in ((0, 1), (1, 3)):
+                k, to = along(h, d)
+                dst = s1.at[n % 4, h, side]
+                out.append(
+                    remote(block(n, h, k, pl.ds(0, 4)), dst, s1_s.at[n, h, side], s1_r.at[n, h, side], to)
+                )
         return out
 
     def second_copies(n):
@@ -402,17 +431,28 @@
 
     def core_add(n):
         core_copy(n).wait_recv()
-        if n >= 2:
-            for copy in first_copies(n - 2):
+        if n >= 3:
+            for copy in opposite_copies(n - 3) + first_copies(n - 3):
                 copy.wait_send()
 
         def add(i, carry):
             for h in range(2):
                 lanes = slice(h * 128, (h + 1) * 128)
-                qbuf[n % 2, h, i] = pbuf[n % 2, c, i, :, :, lanes] + cr[n % 4, i, :, :, lanes]
+                qbuf[n % 3, h, i] = pbuf[n % 2, c, i, :, :, lanes] + cr[n % 4, i, :, :, lanes]
             return carry
 
         lax.fori_loop(0, 4, add, 0)
+        for copy in opposite_copies(n):
+            copy.start()
+
+    def opposite_add(n):
+        for copy in opposite_copies(n):
+            copy.wait_recv()
+        for i in range(2):
+            qbuf[n % 3, 0, i, rem(x + 1, 4)] += so[n % 4, 0, 0, i]
+            qbuf[n % 3, 0, 2 + i, rem(x + 3, 4)] += so[n % 4, 0, 1, i]
+            qbuf[n % 3, 1, rem(y + 1, 4), i] += so[n % 4, 1, 0, i]
+            qbuf[n % 3, 1, rem(y + 3, 4), 2 + i] += so[n % 4, 1, 1, i]
         for copy in first_copies(n):
             copy.start()
 
@@ -425,8 +465,8 @@
 
         def add(i, carry):
             for h in range(2):
-                own = qbuf[n % 2, h, i, x] if h == 0 else qbuf[n % 2, h, y, i]
-                rbuf[n % 2, h, i] = own + s1[n % 4, h, 0, i] + s1[n % 4, h, 1, i] + s1[n % 4, h, 2, i]
+                own = qbuf[n % 3, h, i, x] if h == 0 else qbuf[n % 3, h, y, i]
+                rbuf[n % 2, h, i] = own + s1[n % 4, h, 0, i] + s1[n % 4, h, 1, i]
             return carry
 
         lax.fori_loop(0, 4, add, 0)
@@ -444,19 +484,24 @@
             mixed_ref[:, lanes] = (hid_ref[:, lanes].astype(F32) + total).astype(BF16)
 
     pieces = WIDTH // PIECE
-    for n in range(pieces + 3):
+    for n in range(pieces + 4):
         if n < pieces:
             expand(n)
         if 1 <= n < pieces + 1:
             core_add(n - 1)
         if 2 <= n < pieces + 2:
-            first_add(n - 2)
-        if n >= 3:
-            finish(n - 3)
+            opposite_add(n - 2)
+        if 3 <= n < pieces + 3:
+            first_add(n - 3)
+        if n >= 4:
+            finish(n - 4)
 
     for n in (pieces - 2, pieces - 1):
         core_copy(n).wait_send()
-        for copy in first_copies(n) + second_copies(n):
+        for copy in second_copies(n):
+            copy.wait_send()
+    for n in (pieces - 3, pieces - 2, pieces - 1):
+        for copy in opposite_copies(n) + first_copies(n):
             copy.wait_send()
     for copy in token_1 + token_2 + token_c:
         copy.wait_send()
@@ -561,10 +606,11 @@
             pltpu.VMEM((2, 8, 256, FF), BF16),
             pltpu.VMEM((2, 8, 256, 128), F32),
             pltpu.VMEM((2, 2, 4, 4, ROWS, PIECE), F32),
-            pltpu.VMEM((2, 2, 4, 4, ROWS, 128), F32),
+            pltpu.VMEM((3, 2, 4, 4, ROWS, 128), F32),
             pltpu.VMEM((2, 2, 4, ROWS, 128), F32),
             pltpu.VMEM((4, 4, 4, ROWS, PIECE), F32),
-            pltpu.VMEM((4, 2, 3, 4, ROWS, 128), F32),
+            pltpu.VMEM((4, 2, 2, 2, ROWS, 128), F32),
+            pltpu.VMEM((4, 2, 2, 4, ROWS, 128), F32),
             pltpu.VMEM((4, 2, 3, ROWS, 128), F32),
             dma((3,)),
             dma((3, 4)),
@@ -574,8 +620,10 @@
             dma((16,)),
             dma((8,)),
             dma((8,)),
-            dma((8, 2, 3)),
-            dma((8, 2, 3)),
+            dma((8, 2, 2)),
+            dma((8, 2, 2)),
+            dma((8, 2, 2)),
+            dma((8, 2, 2)),
             dma((8, 2, 3)),
             dma((8, 2, 3)),
         ],

time: 236 us -> 211 us (0.89)
  Pallas kernels: 219 us -> 195 us
    pallas_call x1, Pallas kernels: 219 us -> 195 us  [body(): pl.pallas_call(kernel, out_shape=(jax.ShapeDtypeStruct((ROWS, width), BF1...]
where the time goes in v3:
time: 211 us; the launch traced here: 209 us
  Pallas kernels  195 us (92%)
  local copies, waits for them, and re-layouts  9.78 us (5%)
  other arithmetic  3.58 us (2%)
    pallas_call x1, Pallas kernels, body(): pl.pallas_call(kernel, out_shape=(jax.ShapeDtypeStruct((ROWS, width), BF1...  195 us
    unnamed x28, local copies, waits for them, and re-layouts  4.87 us

profile of v3, /device:TPU:1, one launch (start us, length us, event | category | flops | bytes accessed | tf_op | source)
XLA Modules:
  0.0 208.9 jit_solution(16227525649938485912)
XLA Ops:
  0.6 0.0 copy-start.9
  0.6 0.6 copy-done.9
  1.3 0.0 copy-start.10
  1.3 0.1 convert_reduce_fusion.1
  1.4 0.5 copy-done.10
  1.9 0.1 select_reduce_fusion.2
  2.0 1.1 fusion.4
  3.1 0.0 copy-start.7
  3.1 0.0 copy-start.8
  3.2 0.7 copy-done.7
  3.8 0.0 copy-done.8
  3.9 0.0 copy-start.5
  3.9 0.1 copy.28
  4.0 0.6 copy-done.5
  4.6 0.1 copy.26
  4.7 0.2 select_reduce_fusion
  4.9 0.0 copy-start.6
  4.9 0.2 fusion.7
  5.1 0.5 copy-done.6
  5.6 0.1 copy.27
  5.7 0.0 copy-start.3
  5.7 0.2 select_reduce_fusion.1
  5.9 0.0 copy-start
  5.9 0.4 fusion.8
  6.3 0.4 convert_reduce_fusion
  6.7 0.0 copy-done.3
  6.7 0.0 copy-start.4
  6.7 0.1 copy.39
  6.8 0.8 copy-done.4
  7.5 0.1 copy.38
  7.6 0.0 copy-done
  7.6 0.1 fusion.6
  7.8 0.7 pad_maximum_fusion
  8.5 0.0 copy-start.1
  8.5 0.9 pad.8.nv_ref
  9.4 0.9 pad.7.nk_ref
  10.2 0.0 copy-done.1
  10.2 0.1 copy.33
  10.3 0.9 copy.37
  11.3 194.8 %shard_map.176 = (bf16[64,2048]{1,0:T(8,128)(2,1)}, bf16[32,4,16,128]{3,2,1,0:T(8,128)(2,1)}) custom-call(s32[64]{0:T(128)} %te_ref.1, s32[32]{0:T(128)} %len_ref.1, bf16[64,2176]{1,0:T(8,128)(2,1)} %bitcast.29, bf16[64,2048]{1,0:T(8,128)(2,1)} %bitcast.25, bf16[1,256,384]{2,1,0:T(8,128)(2,1)} %wg_ref.1, bf16[1,256,384]{2,1,0:T(8,128)(2,1)} %wu_ref.1, ...), custom_call_target="tpu_custom_call" | custom-call | flops 20000000000 | bytes 8000000 | tf_op jit(solution)/shard_map/pallas_call | solution.py:593
  206.0 1.1 copy.32
  207.2 0.0 copy-start.2
  207.2 1.0 reshape.95
  208.2 0.0 copy-done.2
  208.2 0.7 copy.41
  (7 shorter events, 0.1 us)
Async XLA Ops:
  0.6 0.7 copy-start.9
  1.3 0.7 copy-start.10
  3.1 0.7 copy-start.7
  3.1 0.7 copy-start.8
  3.9 0.7 copy-start.5
  4.9 0.7 copy-start.6
  5.7 1.0 copy-start.3
  5.9 1.7 copy-start
  6.7 0.8 copy-start.4
  8.5 1.7 copy-start.1
  207.2 1.0 copy-start.2
